TPU v7x, 256 devices: a whole 4x4x8 slice. The times are simulated.
256 devices in a mesh: row: 16 (over y, z_lo, core), col: 16 (over x, z_hi).
Axes of the slice: x: 4, y: 4, z: 8 (z_hi: 4, z_lo: 2; z = z_hi * 2 + z_lo), core: 2. Of those that a mesh axis runs over, the one named last changes fastest.
Arguments:
- genotypes: int32 [18432, 512], P(('row', 'col')), may hold values from 0 to 2, as said below
- allele_counts: int32 [512], replicated, may hold values from 2168 to 106248
- relatedness: float32 [18432, 18432], P('row', 'col'), may hold values from -0.3 to 0.3
- protein_traits: float32 [18432, 128], P(('row', 'col')), may hold values from -6 to 6
Outputs:
- relatedness_out: float32 [18432, 18432], P('row', 'col')
- projected: float32 [18432, 128], P(('row', 'col'))
- cross_products: float32 [128, 128], replicated
Inputs may be any that keep to these rules, and one draw needn't show every extreme that they name: `genotypes`: each dosage is the number of two independent draws that carry the alternative allele, each with the SNP's frequency.
All inputs are finite; a program needn't handle non-finite values.
Results may differ from a plain program's by a relative error of at most 0.00014.
Values sent between devices are 32-bit elements; how exact they have to be, the bound alone decides.
A program may use at most 64 MiB of HBM per device.

v0:
```python
import math

import jax
import jax.numpy as jnp
from jax import lax
from jax.sharding import PartitionSpec as P

SNPS = 512
COHORT = 54208


def broadcast(value, axis, source):
    kept = jnp.where(lax.axis_index(axis) == source, value, 0).astype(value.dtype)
    return lax.psum(kept, axis)


def on_device(genotypes, allele_counts, relatedness, protein_traits):
    frequency = allele_counts.astype(jnp.float32) / (2.0 * COHORT)
    spread = lax.rsqrt(2.0 * frequency * (1.0 - frequency))
    scores = (genotypes.astype(jnp.float32) - 2.0 * frequency) * spread
    block_rows = scores.shape[0]
    snp_count = scores.shape[1]
    joined = jnp.concatenate([scores, protein_traits], axis=1)
    row_count = lax.axis_size("row")
    col_count = lax.axis_size("col")
    col_index = lax.axis_index("col")
    fanout = col_count // row_count
    source = col_index // fanout
    contract = (((1,), (1,)), ((), ()))
    row_panel = lax.all_gather(joined, "col", axis=0, tiled=True)
    root_panel = broadcast(row_panel, "row", source)
    col_scores = root_panel[:, :snp_count]
    col_traits = root_panel[:, snp_count:]
    updated = (
        relatedness
        + lax.dot_general(
            row_panel[:, :snp_count],
            col_scores,
            contract,
            precision=lax.Precision.HIGHEST,
            preferred_element_type=jnp.float32,
        )
        / SNPS
    )
    partial_sum = jnp.dot(
        updated, col_traits, precision=lax.Precision.HIGHEST, preferred_element_type=jnp.float32
    )
    summed = lax.psum(partial_sum, "col")
    own_rows = lax.dynamic_slice_in_dim(summed, col_index * block_rows, block_rows, 0)
    samples = block_rows * row_count * col_count
    projected = own_rows * math.sqrt(snp_count / samples)
    local_cross = lax.dot_general(
        protein_traits,
        own_rows,
        (((0,), (0,)), ((), ())),
        precision=lax.Precision.HIGHEST,
        preferred_element_type=jnp.float32,
    )
    cross_prod = lax.psum(local_cross, ("row", "col")) / samples
    return (updated, projected, cross_prod)


def solution(mesh):
    in_specs = (P(("row", "col"), None), P(), P("row", "col"), P(("row", "col"), None))
    out_specs = (P("row", "col"), P(("row", "col"), None), P())
    return jax.shard_map(
        on_device, mesh=mesh, in_specs=in_specs, out_specs=out_specs, check_vma=False
    )
```

profile of v0, /device:TPU:1, one launch (start us, length us, event | category | flops | bytes accessed | tf_op | source)
XLA Modules:
  0.0 653.8 jit_solution(1538508221447060367)
XLA Ops:
  7.2 0.0 all-gather.2.cloned.1.call-start
  7.2 0.7 convert_multiply_fusion
  7.9 0.9 subtract_multiply_fusion
  8.8 1.5 pad_maximum_fusion
  10.3 0.0 all-gather.2.cloned.1.call-update
  10.3 0.0 all-reduce.4.cloned.1.call-start
  10.4 70.5 %all-gather.2.cloned.1.call-done = f32[1152,640]{1,0:T(8,128)} async-done(((f32[72,640]{1,0:T(8,128)}), f32[1152,640]{1,0:T(8,128)}) %all-gather.2.cloned.1.call-update) | async-done | bytes 2949136 | tf_op jit(solution)/shard_map/all_gather | solution.py:30
  80.9 1.8 broadcast_select_fusion
  82.7 0.0 copy-start.1
  82.7 0.0 all-reduce.4.cloned.1.call-update
  82.7 0.0 all-reduce.6.cloned.1.call-start
  82.7 131.8 %all-reduce.4.cloned.1.call-done = f32[1152,640]{1,0:T(8,128)} async-done(((f32[1152,640]{1,0:T(8,128)}), f32[1152,640]{1,0:T(8,128)}) %all-reduce.4.cloned.1.call-update) | async-done | bytes 2949136 | tf_op jit(solution)/shard_map/psum | solution.py:14
  214.5 0.0 copy-done.1
  214.5 12.7 %fusion = f32[1152,1152]{1,0:T(8,128)S(1)} fusion(f32[1152,1152]{1,0:T(8,128)} %param.6, f32[1152,640]{1,0:T(8,128)} %all-reduce.4.cloned.1.call-done, f32[1152,640]{1,0:T(8,128)S(1)} %copy-done.1), kind=kOutput, calls=%fused_computation.1 | convolution fusion | flops 8156381184 | bytes 15335424 | tf_op jit(solution)/shard_map/dot_general | solution.py:36
  227.2 0.0 copy-start
  227.2 2.4 copy-done
  229.6 0.0 copy-start.2
  229.6 6.4 fusion.3
  235.9 0.0 all-reduce.6.cloned.1.call-update
  236.0 0.0 all-reduce.8.cloned.1.call-start
  236.0 158.8 %all-reduce.6.cloned.1.call-done = f32[1152,128]{1,0:T(8,128)} async-done(((f32[1152,128]{1,0:T(8,128)}), f32[1152,128]{1,0:T(8,128)}) %all-reduce.6.cloned.1.call-update) | async-done | bytes 589840 | tf_op jit(solution)/shard_map/psum | solution.py:48
  394.8 0.0 copy-done.2
  394.8 1.7 convolution_bitcast_fusion
  396.5 0.0 all-reduce.8.cloned.1.call-update
  396.5 1.4 dynamic-slice_multiply_fusion
  397.9 247.7 %all-reduce.8.cloned.1.call-done = f32[128,128]{0,1:T(8,128)} async-done(((f32[128,128]{0,1:T(8,128)}), f32[128,128]{0,1:T(8,128)}) %all-reduce.8.cloned.1.call-update) | async-done | bytes 65552 | tf_op jit(solution)/shard_map/psum | solution.py:59
  645.7 0.8 broadcast_multiply_fusion
  646.5 0.7 copy.7
Async XLA Ops:
  7.2 73.7 %all-gather.2.cloned.1.call-start = ((), (), s32[]{:S(2)}) async-start(), calls=%async_computation | async-start | bytes 3133440 | tf_op jit(solution)/shard_map/all_gather | solution.py:30
  10.3 204.2 %all-reduce.4.cloned.1.call-start = ((), (), s32[]{:S(2)}) async-start(), calls=%async_computation.1 | async-start | bytes 5898240 | tf_op jit(solution)/shard_map/psum | solution.py:14
  82.7 131.9 %copy-start.1 = (f32[1152,640]{1,0:T(8,128)S(1)}, f32[1152,640]{1,0:T(8,128)}, u32[]{:S(2)}) copy-start(f32[1152,640]{1,0:T(8,128)} %all-gather.2.cloned.1.call-done) | copy-start | bytes 8847364
  82.7 312.2 %all-reduce.6.cloned.1.call-start = ((), (), s32[]{:S(2)}) async-start(), calls=%async_computation.2 | async-start | bytes 1179648 | tf_op jit(solution)/shard_map/psum | solution.py:48
  227.2 2.4 copy-start
  229.6 165.3 %copy-start.2 = (f32[72,128]{1,0:T(8,128)S(1)}, f32[72,128]{1,0:T(8,128)}, u32[]{:S(2)}) copy-start(f32[72,128]{1,0:T(8,128)} %param.7) | copy-start | bytes 110596
  236.0 409.7 %all-reduce.8.cloned.1.call-start = ((), (), s32[]{:S(2)}) async-start(), calls=%async_computation.3 | async-start | bytes 131072 | tf_op jit(solution)/shard_map/psum | solution.py:59
Sparse Core Ops, SparseCore 0:
  11.1 69.7 all-gather.1
  84.1 130.3 all-reduce.3
  236.1 158.6 all-reduce.5
  401.7 243.9 all-reduce.7
where the time goes:
time: 654 us
  waiting for transfers between devices  609 us (93%)
  matrix products  20.7 us (3%)
  between operations  13.8 us (2%)
  other arithmetic  7.11 us (1%)
    psum x1, waiting for transfers between devices, on_device(): cross_prod = lax.psum(local_cross, ('row', 'col')) / samples  248 us
    psum x1, waiting for transfers between devices, on_device(): summed = lax.psum(partial_sum, 'col')  159 us
    psum x1, waiting for transfers between devices, broadcast(): return lax.psum(kept, axis)  132 us
    all_gather x1, waiting for transfers between devices, on_device(): row_panel = lax.all_gather(joined, 'col', axis=0, tiled=True)  70.5 us
  transfers between devices with their start and end apart: 4, of which 4 were waited for; matrix products, arithmetic and copies ran while one was open for 0% of the time, Pallas kernels for 0%

commit v1 on v0

v1 whole, which is shorter than its diff:
```python
import itertools
import math

import jax
import jax.numpy as jnp
from jax import lax
from jax.experimental import pallas as pl
from jax.experimental.pallas import tpu as pltpu
from jax.sharding import PartitionSpec as P

SNPS = 512
PROT = 128
COHORT = 54208
ROWS = 72
TOP = 40
GROUP = 4 * ROWS
PANEL = 16 * ROWS
SAMPLES = 16 * PANEL
MESH = pl.DeviceIdType.MESH
HIGHEST = lax.Precision.HIGHEST
F32 = jnp.float32
BF16 = jnp.bfloat16
NSEM = 128


def dot(a, b, contract, precision=None):
    return lax.dot_general(
        a, b, (contract, ((), ())), precision=precision, preferred_element_type=F32
    )


def split(value):
    high = value.astype(BF16)
    return high, (value - high.astype(F32)).astype(BF16)


def aligned(start, size, unit=8):
    return pl.ds(pl.multiple_of(start, unit), size)


def snp_tables(counts):
    frequency = counts.astype(F32) / (2.0 * COHORT)
    spread = lax.rsqrt(2.0 * frequency * (1.0 - frequency))
    return frequency, spread


def exchange_kernel(
    counts_ref,
    geno_ref,
    traits_ref,
    rel_ref,
    high_ref,
    low_ref,
    shift_ref,
    plain_ref,
    product_ref,
    cross_ref,
    rowp,
    colp,
    tp,
    rel,
    zbuf,
    zsum,
    rsx,
    rsz,
    gsrc,
    gk,
    ga,
    g7,
    gz,
    gx,
    gres,
    csrc,
    ck,
    ca,
    c7,
    cz,
    cx,
    cres,
    ssem,
    rsem,
    lsem,
):
    r = lax.axis_index("row")
    c = lax.axis_index("col")
    y, zl, core = r // 4, (r // 2) % 2, r % 2
    x, zh = c // 4, c % 4

    def row_of(y_, zl_, core_):
        return y_ * 4 + zl_ * 2 + core_

    def at_x(step):
        return (r, ((x + step) % 4) * 4 + zh)

    def at_z(step):
        return (r, x * 4 + (zh + step) % 4)

    def at_y(dy, dl):
        return (row_of((y + dy) % 4, (zl + dl) % 2, core), c)

    sibling = (row_of(y, zl, 1 - core), c)
    mirror = (c, r)
    others = [(dy, dl) for dl in range(2) for dy in range(4) if (dy, dl) != (0, 0)]
    partners = (
        [sibling]
        + [at_y(dy, dl) for dy, dl in others]
        + [at_x(i) for i in (1, 2, 3)]
        + [at_z(i) for i in (1, 2, 3)]
    )
    far = r != c

    names = itertools.count()
    started = []

    def copy(number, src, dst, to):
        return pltpu.make_async_remote_copy(
            src_ref=src,
            dst_ref=dst,
            send_sem=ssem.at[number],
            recv_sem=rsem.at[number],
            device_id=to,
            device_id_type=MESH,
        )

    def send(src, dst, to):
        number = next(names)
        moved = copy(number, src, dst, to)
        moved.start()
        started.append(moved)
        return number

    def arrived(number, landing):
        copy(number, landing, landing, sibling).wait_recv()

    load_rel = pltpu.make_async_copy(rel_ref, rel, lsem.at[0])
    load_rel.start()
    keep_own = pltpu.make_async_copy(geno_ref, rowp.at[c], lsem.at[1])
    keep_own.start()

    barrier = pltpu.get_barrier_semaphore()
    for to in partners:
        pl.semaphore_signal(barrier, inc=1, device_id=to, device_id_type=MESH)

    @pl.when(far)
    def _():
        pl.semaphore_signal(barrier, inc=1, device_id=mirror, device_id_type=MESH)

    frequency, spread = snp_tables(counts_ref[...])
    scores = (geno_ref[...].astype(F32) - 2.0 * frequency) * spread
    gsrc[...] = dot(traits_ref[...], scores, ((0,), (0,)), HIGHEST)

    pl.semaphore_wait(barrier, len(partners) + far.astype(jnp.int32))

    m_traits, m_geno = next(names), next(names)

    @pl.when(far)
    def _():
        copy(m_traits, traits_ref, tp.at[c], mirror).start()
        copy(m_geno, geno_ref, colp.at[c], mirror).start()

    @pl.when(jnp.logical_not(far))
    def _():
        for src, dst, sem in ((traits_ref, tp.at[c], 2), (geno_ref, colp.at[c], 3)):
            pltpu.make_async_copy(src, dst, lsem.at[sem]).start()

    def mirrored(number, src, landing, sem):
        @pl.when(far)
        def _():
            moved = copy(number, src, landing, mirror)
            moved.wait_recv()

        @pl.when(jnp.logical_not(far))
        def _():
            pltpu.make_async_copy(src, landing, lsem.at[sem]).wait()

    class Total:
        def __init__(self, src, bk, acc, b7, bz, bx, res, halves):
            self.src, self.bk, self.acc, self.b7 = src, bk, acc, b7
            self.bz, self.bx, self.res = bz, bx, res
            self.halves = halves
            self.rows = 64 if halves else 128
            self.chunk = self.rows // 8
            self.base = core * 64 if halves else 0

        def part(self, index):
            return aligned(index * self.chunk, self.chunk)

        def to_core(self):
            first = (1 - core) * 64 if self.halves else 0
            self.n_core = send(self.src.at[aligned(first, self.rows)], self.bk, sibling)

        def to_row(self):
            arrived(self.n_core, self.bk)
            mine = self.src[aligned(self.base, self.rows), :]
            self.acc[...] = mine + self.bk[...]
            me = y * 2 + zl
            self.n_row = []
            for dy, dl in others:
                q = ((y + dy) % 4) * 2 + (zl + dl) % 2
                self.n_row.append(
                    send(self.acc.at[self.part(q)], self.b7.at[me], at_y(dy, dl))
                )

        def to_z(self):
            me = y * 2 + zl
            for number in self.n_row:
                arrived(number, self.b7.at[me])
            self.b7[me] = self.acc[self.part(me), :]
            total = self.b7[0]
            for i in range(1, 8):
                total = total + self.b7[i]
            self.bz[zh] = total
            self.n_z = [send(self.bz.at[zh], self.bz.at[zh], at_z(i)) for i in (1, 2, 3)]

        def to_x(self):
            for number in self.n_z:
                arrived(number, self.bz.at[zh])
            total = (self.bz[0] + self.bz[1]) + (self.bz[2] + self.bz[3])
            self.bx[x] = total
            self.n_x = [send(self.bx.at[x], self.bx.at[x], at_x(i)) for i in (1, 2, 3)]

        def back_row(self):
            for number in self.n_x:
                arrived(number, self.bx.at[x])
            total = (self.bx[0] + self.bx[1]) + (self.bx[2] + self.bx[3])
            me = y * 2 + zl
            mine = aligned(self.base + me * self.chunk, self.chunk)
            self.res[mine, :] = total
            self.n_back = [
                send(self.res.at[mine], self.res.at[mine], at_y(dy, dl)) for dy, dl in others
            ]

        def back_core(self):
            me = y * 2 + zl
            mine = aligned(self.base + me * self.chunk, self.chunk)
            for number in self.n_back:
                arrived(number, self.res.at[mine])
            if self.halves:
                half = aligned(self.base, 64)
                self.n_half = send(self.res.at[half], self.res.at[half], sibling)

        def done(self):
            if self.halves:
                arrived(self.n_half, self.res.at[aligned(self.base, 64)])

    gram = Total(gsrc, gk, ga, g7, gz, gx, gres, True)
    cross = Total(csrc, ck, ca, c7, cz, cx, cres, False)

    def slot(x_step, z_step):
        return ((x + x_step) % 4) * 4 + (zh + z_step) % 4

    n_zup = send(geno_ref, rowp.at[c], at_z(1))
    n_zdown = send(geno_ref, rowp.at[c], at_z(3))
    n_xup, n_xdown = {}, {}

    def x_send(k, src):
        there = rowp.at[slot(0, k)]
        n_xup[k] = send(src, there, at_x(1))
        n_xdown[k] = send(src, there, at_x(3))

    x_send(0, geno_ref)
    gram.to_core()

    n_xfup, n_xfdown = {}, {}

    def x_forward(k):
        low = rowp.at[slot(3, k)]
        arrived(n_xup[k], low)
        n_xfup[k] = send(low.at[0:TOP], low.at[0:TOP], at_x(1))
        high = rowp.at[slot(1, k)]
        arrived(n_xdown[k], high)
        n_xfdown[k] = send(high.at[TOP:ROWS], high.at[TOP:ROWS], at_x(3))

    def x_last(k):
        opposite = rowp.at[slot(2, k)]
        arrived(n_xfup[k], opposite.at[0:TOP])
        arrived(n_xfdown[k], opposite.at[TOP:ROWS])

    def cslot(dy, dl, other=0):
        return row_of((y + dy) % 4, (zl + dl) % 2, (core + other) % 2)

    n_yup, n_ydown, n_yfup, n_yfdown, n_pair = {}, {}, {}, {}, {}

    def pair_send(dy, dl):
        block = colp.at[cslot(dy, dl)]
        n_pair[dy, dl] = send(block, block, sibling)

    def y_send(dl):
        block = colp.at[cslot(0, dl)]
        n_yup[dl] = send(block, block, at_y(1, 0))
        n_ydown[dl] = send(block, block, at_y(3, 0))
        pair_send(0, dl)

    def y_forward(dl):
        low = colp.at[cslot(3, dl)]
        arrived(n_yup[dl], low)
        n_yfup[dl] = send(low.at[0:TOP], low.at[0:TOP], at_y(1, 0))
        high = colp.at[cslot(1, dl)]
        arrived(n_ydown[dl], high)
        n_yfdown[dl] = send(high.at[TOP:ROWS], high.at[TOP:ROWS], at_y(3, 0))
        pair_send(3, dl)
        pair_send(1, dl)

    def y_last(dl):
        opposite = colp.at[cslot(2, dl)]
        arrived(n_yfup[dl], opposite.at[0:TOP])
        arrived(n_yfdown[dl], opposite.at[TOP:ROWS])
        pair_send(2, dl)

    mirrored(m_traits, traits_ref, tp.at[r], 2)
    n_t = [send(tp.at[r], tp.at[r], at_y(dy, dl)) for dy, dl in others]
    n_tp = {(0, 0): send(tp.at[r], tp.at[r], sibling)}

    gram.to_row()

    mirrored(m_geno, geno_ref, colp.at[r], 3)
    n_zl = send(colp.at[r], colp.at[r], at_y(0, 1))
    y_send(0)

    low = rowp.at[slot(0, 3)]
    arrived(n_zup, low)
    n_zfup = send(low.at[0:TOP], low.at[0:TOP], at_z(1))
    x_send(3, low)
    high = rowp.at[slot(0, 1)]
    arrived(n_zdown, high)
    n_zfdown = send(high.at[TOP:ROWS], high.at[TOP:ROWS], at_z(3))
    x_send(1, high)

    for number, (dy, dl) in zip(n_t, others, strict=True):
        block = tp.at[cslot(-dy, -dl)]
        arrived(number, block)
        n_tp[-dy % 4, dl] = send(block, block, sibling)

    gram.to_z()

    arrived(n_zl, colp.at[cslot(0, 1)])
    y_send(1)
    x_forward(0)

    for (dy, dl), number in n_tp.items():
        arrived(number, tp.at[cslot(dy, dl, 1)])
    load_rel.wait()
    t_all = tp[...].reshape(PANEL, PROT)
    t_high, t_low = split(t_all)
    t_both = jnp.concatenate([t_high, t_low], axis=1)

    def times_traits(step, _):
        there = (x + step) % 4
        rows = aligned(there * GROUP, GROUP)
        r_high, r_low = split(rel[rows, :])
        both = dot(r_high, t_both, ((1,), (0,)))
        zbuf[rows, :] = (
            both[:, :PROT] + both[:, PROT:] + dot(r_low, t_high, ((1,), (0,)))
        )
        return 0

    lax.fori_loop(0, 4, times_traits, 0)
    n_rsx = []
    for i in (1, 2, 3):
        rows = aligned(((x + i) % 4) * GROUP, GROUP)
        n_rsx.append(send(zbuf.at[rows], rsx.at[x], at_x(i)))

    opposite = rowp.at[slot(0, 2)]
    arrived(n_zfup, opposite.at[0:TOP])
    arrived(n_zfdown, opposite.at[TOP:ROWS])
    x_send(2, opposite)
    y_forward(0)
    y_forward(1)
    gram.to_x()
    x_forward(3)
    x_forward(1)
    y_last(0)
    y_last(1)

    rsx[x] = zbuf[aligned(x * GROUP, GROUP), :]
    for number in n_rsx:
        arrived(number, rsx.at[x])
    summed = (rsx[0] + rsx[1]) + (rsx[2] + rsx[3])
    zsum[...] = summed
    n_rsz = []
    for i in (1, 2, 3):
        rows = aligned(((zh + i) % 4) * ROWS, ROWS)
        n_rsz.append(send(zsum.at[rows], rsz.at[zh], at_z(i)))
    rsz[zh] = zsum[aligned(zh * ROWS, ROWS), :]

    gram.back_row()
    x_forward(2)
    for dl in range(2):
        for dy in range(4):
            arrived(n_pair[dy, dl], colp.at[cslot(dy, dl, 1)])
    gram.back_core()

    for number in n_rsz:
        arrived(number, rsz.at[zh])
    own = (rsz[0] + rsz[1]) + (rsz[2] + rsz[3])
    csrc[...] = dot(traits_ref[...], own, ((0,), (0,)), HIGHEST)
    cross.to_core()

    keep_own.wait()
    nearest = jnp.round(2.0 * frequency)
    offset = 2.0 * frequency - nearest
    weight = spread * spread * (1.0 / SNPS)

    def plain(step, _):
        block = colp[pl.ds(4 * step, 4)].reshape(GROUP, SNPS).astype(F32)
        plain_ref[aligned(step * GROUP, GROUP, 16), :] = (block - nearest).astype(BF16)
        return 0

    lax.fori_loop(0, 4, plain, 0)

    cross.to_row()

    def weighted(step):
        which = (x + step) % 4
        rows = aligned(which * GROUP, GROUP, 16)
        block = rowp[pl.ds(4 * which, 4)].reshape(GROUP, SNPS).astype(F32)
        value = ((block - nearest) - offset) * weight
        one, two = split(value)
        high_ref[rows, :] = one
        low_ref[rows, :] = two
        shift = jnp.sum(value * offset, axis=1, keepdims=True)
        shift_ref[rows, :] = jnp.broadcast_to(shift, (GROUP, PROT))

    weighted(0)
    cross.to_z()
    weighted(1)
    weighted(3)
    gram.done()
    cross.to_x()
    for k in (0, 3, 1, 2):
        x_last(k)
    weighted(2)
    cross.back_row()
    product_ref[...] = own + dot(scores, gres[...], ((1,), (1,)), HIGHEST) * (1.0 / SNPS)
    whole = gres[...]
    squares = dot(whole, whole, ((1,), (1,)), HIGHEST) * (1.0 / SNPS)
    cross.back_core()
    cross.done()
    cross_ref[...] = cres[...] + squares

    for moved in started:
        moved.wait_send()

    @pl.when(far)
    def _():
        copy(m_traits, traits_ref, tp.at[c], mirror).wait_send()
        copy(m_geno, geno_ref, colp.at[c], mirror).wait_send()


def update_kernel(
    rel_ref, high_ref, low_ref, shift_ref, plain_ref, product_ref, cross_ref, out_ref, proj_ref, cp_ref
):
    plain = plain_ref[...]
    sums = dot(high_ref[...], plain, ((1,), (1,))) + dot(low_ref[...], plain, ((1,), (1,)))
    out_ref[...] = rel_ref[...] + (sums - shift_ref[:, 0:1])
    proj_ref[...] = product_ref[...] * math.sqrt(SNPS / SAMPLES)
    cp_ref[...] = cross_ref[...] * (1.0 / SAMPLES)


def on_device(genotypes, allele_counts, relatedness, protein_traits):
    vmem = pl.BlockSpec(memory_space=pltpu.VMEM)
    anywhere = pl.BlockSpec(memory_space=pl.ANY)
    like = jax.ShapeDtypeStruct
    f32 = lambda *shape: pltpu.VMEM(shape, F32)
    high, low, shift, plain, product, cross = pl.pallas_call(
        exchange_kernel,
        out_shape=(
            like((PANEL, SNPS), BF16),
            like((PANEL, SNPS), BF16),
            like((PANEL, PROT), F32),
            like((PANEL, SNPS), BF16),
            like((ROWS, PROT), F32),
            like((PROT, PROT), F32),
        ),
        in_specs=[vmem, vmem, vmem, anywhere],
        out_specs=(vmem,) * 6,
        scratch_shapes=[
            pltpu.VMEM((16, ROWS, SNPS), jnp.int32),
            pltpu.VMEM((16, ROWS, SNPS), jnp.int32),
            f32(16, ROWS, PROT),
            f32(PANEL, PANEL),
            f32(PANEL, PROT),
            f32(GROUP, PROT),
            f32(4, GROUP, PROT),
            f32(4, ROWS, PROT),
            f32(128, SNPS),
            f32(64, SNPS),
            f32(64, SNPS),
            f32(8, 8, SNPS),
            f32(4, 8, SNPS),
            f32(4, 8, SNPS),
            f32(128, SNPS),
            f32(128, PROT),
            f32(128, PROT),
            f32(128, PROT),
            f32(8, 16, PROT),
            f32(4, 16, PROT),
            f32(4, 16, PROT),
            f32(128, PROT),
            pltpu.SemaphoreType.DMA((NSEM,)),
            pltpu.SemaphoreType.DMA((NSEM,)),
            pltpu.SemaphoreType.DMA((4,)),
        ],
        compiler_params=pltpu.CompilerParams(
            collective_id=1, has_side_effects=True, vmem_limit_bytes=48 * 2**20
        ),
        name="exchange",
    )(allele_counts.reshape(1, SNPS), genotypes, protein_traits, relatedness)
    steps = 4
    tile = PANEL // steps
    rows = lambda width: pl.BlockSpec((tile, width), lambda i: (i, 0))
    whole = lambda *shape: pl.BlockSpec(shape, lambda i: (0, 0))
    return pl.pallas_call(
        update_kernel,
        grid=(steps,),
        out_shape=(
            like((PANEL, PANEL), F32),
            like((ROWS, PROT), F32),
            like((PROT, PROT), F32),
        ),
        in_specs=[
            rows(PANEL),
            rows(SNPS),
            rows(SNPS),
            rows(PROT),
            whole(PANEL, SNPS),
            whole(ROWS, PROT),
            whole(PROT, PROT),
        ],
        out_specs=(rows(PANEL), whole(ROWS, PROT), whole(PROT, PROT)),
        compiler_params=pltpu.CompilerParams(vmem_limit_bytes=48 * 2**20),
        name="update",
    )(relatedness, high, low, shift, plain, product, cross)


def solution(mesh):
    in_specs = (P(("row", "col"), None), P(), P("row", "col"), P(("row", "col"), None))
    out_specs = (P("row", "col"), P(("row", "col"), None), P())
    return jax.shard_map(
        on_device, mesh=mesh, in_specs=in_specs, out_specs=out_specs, check_vma=False
    )
```

time: 654 us -> 83.7 us (0.13)
  waiting for transfers between devices: 609 us -> 0 us
  Pallas kernels: 0 us -> 79.8 us
  matrix products: 20.7 us -> 0 us
  between operations: 13.8 us -> 0.65 us
  other arithmetic: 7.11 us -> 0 us
    psum x3 -> x0, waiting for transfers between devices: 538 us -> none  [the longest x1 248 us: on_device(): cross_prod = lax.psum(local_cross, ('row', 'col')) / samples]
    pallas_call x0 -> x2, Pallas kernels: none -> 79.8 us  [the longest x1 72.5 us: on_device(): pl.pallas_call(exchange_kernel, out_shape=(like((PANEL, SNPS), BF16), lik...]
    all_gather x1 -> x0, waiting for transfers between devices: 70.5 us -> none  [on_device(): row_panel = lax.all_gather(joined, 'col', axis=0, tiled=True)]
    dot_general x3 -> x0, matrix products: 20.7 us -> none  [the longest x1 12.7 us: on_device(): lax.dot_general(row_panel[:, :snp_count], col_scores, contract, precision...]
  transfers between devices with their start and end apart: 4 -> 0, of which waited for: 4 -> 0; matrix products, arithmetic and copies ran while one was open for 0% -> 0% of each run, Pallas kernels for 0% -> 0%
where the time goes in v1:
time: 83.7 us; the launch traced here: 82.8 us
  Pallas kernels  79.8 us (95%)
  local copies, waits for them, and re-layouts  2.35 us (3%)
    pallas_call x1, Pallas kernels, on_device(): pl.pallas_call(exchange_kernel, out_shape=(like((PANEL, SNPS), BF16), lik...  72.5 us
    pallas_call x1, Pallas kernels, on_device(): pl.pallas_call(update_kernel, grid=(steps,), out_shape=(like((PANEL, PANE...  7.3 us
    unnamed x6, local copies, waits for them, and re-layouts  2.35 us

profile of v1, /device:TPU:1, one launch (start us, length us, event | category | flops | bytes accessed | tf_op | source)
XLA Modules:
  0.0 82.8 jit_solution(717700612495510019)
XLA Ops:
  0.6 0.0 copy-start
  0.6 0.9 %copy-done = s32[72,512]{1,0:T(8,128)S(1)} copy-done((s32[72,512]{1,0:T(8,128)S(1)}, s32[72,512]{1,0:T(8,128)}, u32[]{:S(2)}) %copy-start) | copy-done | bytes 147480
  1.5 0.0 copy-start.1
  1.5 0.8 copy-done.1
  2.3 0.0 copy-start.2
  2.3 0.7 copy-done.2
  3.0 72.5 %exchange.1 = (bf16[1152,512]{1,0:T(8,128)(2,1)S(1)}, bf16[1152,512]{1,0:T(8,128)(2,1)S(1)}, f32[1152,128]{1,0:T(8,128)S(1)}, bf16[1152,512]{1,0:T(8,128)(2,1)S(...) custom-call(s32[1,512]{1,0:T(1,128)S(1)} %bitcast.1, s32[72,512]{1,0:T(8,128)S(1)} %copy-done, ...), custom_call_target="tpu_custom_call" | custom-call | tf_op jit(solution)/shard_map/exchange/pallas_call | solution.py:465
  75.5 7.3 %update.1 = (f32[1152,1152]{1,0:T(8,128)}, f32[72,128]{1,0:T(8,128)}, f32[128,128]{1,0:T(8,128)}) custom-call(f32[1152,1152]{1,0:T(8,128)} %rel_ref.3, bf16[1152,512]{1,0:T(8,128)(2,1)S(1)} %get-tuple-element.9.high_ref, bf16[1152,512]{1,0:T(8,128)(2,1)S(1)} %get-tuple-element.10.low_ref, f32[1152,128]{1,0:T(8,128)S(1)} %get-tuple-element.11.shift_ref, ...), custom_call_target="tpu_custom_call" | custom-call | tf_op jit(solution)/shard_map/update/pallas_call | solution.py:513
Async XLA Ops:
  0.6 0.9 %copy-start = (s32[72,512]{1,0:T(8,128)S(1)}, s32[72,512]{1,0:T(8,128)}, u32[]{:S(2)}) copy-start(s32[72,512]{1,0:T(8,128)} %geno_ref.1) | copy-start | bytes 442372
  1.5 0.8 copy-start.1
  2.3 0.7 copy-start.2

commit v2 on v1

v2 whole, which is shorter than its diff:
```python
import itertools
import math

import jax
import jax.numpy as jnp
from jax import lax
from jax.experimental import pallas as pl
from jax.experimental.pallas import tpu as pltpu
from jax.sharding import PartitionSpec as P

SNPS = 512
PROT = 128
COHORT = 54208
ROWS = 72
TOP = 40
GROUP = 4 * ROWS
PANEL = 16 * ROWS
SAMPLES = 16 * PANEL
MESH = pl.DeviceIdType.MESH
HIGHEST = lax.Precision.HIGHEST
F32 = jnp.float32
BF16 = jnp.bfloat16
NSEM = 160
STORES = 8
VMEM_LIMIT = 52 * 2**20
ORDER = (
    "g0", "t0", "z0", "m0", "t1", "g1", "x0", "z1d", "m1", "z1u", "t2", "t3", "m2t", "yf0u",
    "yf0d", "tz0", "g2", "m3t", "m1t", "m2", "yl0", "m0t", "g3", "z2", "t4", "yf1u", "tz1",
    "yf1d", "xf1u", "tc", "s0", "xf3u", "yl1", "g4", "xf0d", "s1", "p", "h", "xf2d", "xf3d",
    "xf2u", "g5", "u0", "xf0u", "u3", "xf1d", "g6", "og", "s2", "u1", "xl0", "xl2", "op", "xl1",
    "xl3", "u2", "s3", "oc",
)


def dot(a, b, contract, precision=None):
    return lax.dot_general(
        a, b, (contract, ((), ())), precision=precision, preferred_element_type=F32
    )


def split(value):
    high = value.astype(BF16)
    return high, (value - high.astype(F32)).astype(BF16)


def aligned(start, size, unit=8):
    return pl.ds(pl.multiple_of(start, unit), size)


def snp_tables(counts):
    frequency = counts.astype(F32) / (2.0 * COHORT)
    spread = lax.rsqrt(2.0 * frequency * (1.0 - frequency))
    return frequency, spread


def exchange_kernel(
    counts_ref,
    geno_ref,
    traits_ref,
    rel_ref,
    rel,
    projected_ref,
    cross_ref,
    counts,
    traits,
    rowp,
    colp,
    tp,
    tr,
    turned,
    tb,
    zbuf,
    zsum,
    rsx,
    rsz,
    gsrc,
    gk,
    ga,
    g7,
    gz,
    gx,
    gres,
    csrc,
    c16,
    cc,
    cres,
    ssem,
    rsem,
    lsem,
):
    r = lax.axis_index("row")
    c = lax.axis_index("col")
    y, zl, core = r // 4, (r // 2) % 2, r % 2
    x, zh = c // 4, c % 4

    def row_of(y_, zl_, core_):
        return y_ * 4 + zl_ * 2 + core_

    def at_x(step):
        return (r, ((x + step) % 4) * 4 + zh)

    def at_z(step):
        return (r, x * 4 + (zh + step) % 4)

    def at_y(dy, dl):
        return (row_of((y + dy) % 4, (zl + dl) % 2, core), c)

    sibling = (row_of(y, zl, 1 - core), c)
    mirror = (c, r)
    others = [(dy, dl) for dl in range(2) for dy in range(4) if (dy, dl) != (0, 0)]

    def at_row(dy, dl, dk):
        return (row_of((y + dy) % 4, (zl + dl) % 2, (core + dk) % 2), c)

    def at_col(dx, dz):
        return (r, ((x + dx) % 4) * 4 + (zh + dz) % 4)

    row_others = [
        (dy, dl, dk) for dk in range(2) for dl in range(2) for dy in range(4)
    ][1:]
    col_others = [(dx, dz) for dz in range(4) for dx in range(4)][1:]
    partners = [at_row(*d) for d in row_others] + [at_col(*d) for d in col_others]
    far = r != c

    names = itertools.count()
    started = []

    def copy(number, src, dst, to):
        return pltpu.make_async_remote_copy(
            src_ref=src,
            dst_ref=dst,
            send_sem=ssem.at[number],
            recv_sem=rsem.at[number],
            device_id=to,
            device_id_type=MESH,
        )

    def send(src, dst, to):
        number = next(names)
        moved = copy(number, src, dst, to)
        moved.start()
        started.append(moved)
        return number

    def arrived(number, landing):
        copy(number, landing, landing, sibling).wait_recv()

    load_counts = pltpu.make_async_copy(counts_ref, counts, lsem.at[4])
    load_counts.start()
    load_traits = pltpu.make_async_copy(traits_ref, traits, lsem.at[5])
    load_traits.start()
    keep_own = pltpu.make_async_copy(geno_ref, rowp.at[c], lsem.at[1])
    keep_own.start()
    load_rel = pltpu.make_async_copy(rel_ref, rel, lsem.at[0])
    load_rel.start()

    barrier = pltpu.get_barrier_semaphore()
    for to in partners:
        pl.semaphore_signal(barrier, inc=1, device_id=to, device_id_type=MESH)

    @pl.when(far)
    def _():
        pl.semaphore_signal(barrier, inc=1, device_id=mirror, device_id_type=MESH)

    load_counts.wait()
    frequency, spread = snp_tables(counts[...])
    nearest = jnp.round(2.0 * frequency)
    offset = 2.0 * frequency - nearest
    weight = spread * spread * (1.0 / SNPS)
    keep_own.wait()
    load_traits.wait()
    scores = (rowp[c].astype(F32) - 2.0 * frequency) * spread
    gsrc[...] = dot(traits[...], scores, ((0,), (0,)), HIGHEST)

    pl.semaphore_wait(barrier, len(partners) + far.astype(jnp.int32))

    steps = {}

    def step(function):
        steps[function.__name__] = function

    m_traits, m_geno = next(names), next(names)
    mirrors = {
        "t": (m_traits, traits_ref, lambda i: tp.at[i], 2),
        "c": (m_geno, geno_ref, lambda i: cblock(i), 3),
    }

    def cblock(index):
        return colp.at[aligned(index * ROWS, ROWS)]

    def mirror_start(which):
        number, src, panel, sem = mirrors[which]

        @pl.when(far)
        def _():
            copy(number, src, panel(c), mirror).start()

        @pl.when(jnp.logical_not(far))
        def _():
            pltpu.make_async_copy(src, panel(c), lsem.at[sem]).start()

    def mirrored(which):
        number, src, panel, sem = mirrors[which]

        @pl.when(far)
        def _():
            copy(number, src, panel(r), mirror).wait_recv()

        @pl.when(jnp.logical_not(far))
        def _():
            pltpu.make_async_copy(src, panel(r), lsem.at[sem]).wait()

    def mirror_sent(which):
        number, src, panel, sem = mirrors[which]

        @pl.when(far)
        def _():
            copy(number, src, panel(c), mirror).wait_send()

    class Total:
        def __init__(self, src, bk, acc, b7, bz, bx, res, halves):
            self.src, self.bk, self.acc, self.b7 = src, bk, acc, b7
            self.bz, self.bx, self.res = bz, bx, res
            self.halves = halves
            self.rows = 64 if halves else 128
            self.chunk = self.rows // 8
            self.base = core * 64 if halves else 0

        def part(self, index):
            return aligned(index * self.chunk, self.chunk)

        def to_core(self):
            first = (1 - core) * 64 if self.halves else 0
            self.n_core = send(self.src.at[aligned(first, self.rows)], self.bk, sibling)

        def to_row(self):
            arrived(self.n_core, self.bk)
            mine = self.src[aligned(self.base, self.rows), :]
            self.acc[...] = mine + self.bk[...]
            me = y * 2 + zl
            self.n_row = []
            for dy, dl in others:
                q = ((y + dy) % 4) * 2 + (zl + dl) % 2
                self.n_row.append(
                    send(self.acc.at[self.part(q)], self.b7.at[me], at_y(dy, dl))
                )

        def to_z(self):
            me = y * 2 + zl
            for number in self.n_row:
                arrived(number, self.b7.at[me])
            self.b7[me] = self.acc[self.part(me), :]
            total = self.b7[0]
            for i in range(1, 8):
                total = total + self.b7[i]
            self.bz[zh] = total
            self.n_z = [send(self.bz.at[zh], self.bz.at[zh], at_z(i)) for i in (1, 2, 3)]

        def to_x(self):
            for number in self.n_z:
                arrived(number, self.bz.at[zh])
            total = (self.bz[0] + self.bz[1]) + (self.bz[2] + self.bz[3])
            self.bx[x] = total
            self.n_x = [send(self.bx.at[x], self.bx.at[x], at_x(i)) for i in (1, 2, 3)]

        def back_row(self):
            for number in self.n_x:
                arrived(number, self.bx.at[x])
            total = (self.bx[0] + self.bx[1]) + (self.bx[2] + self.bx[3])
            me = y * 2 + zl
            mine = aligned(self.base + me * self.chunk, self.chunk)
            self.res[mine, :] = total
            self.n_back = [
                send(self.res.at[mine], self.res.at[mine], at_y(dy, dl)) for dy, dl in others
            ]

        def back_core(self):
            me = y * 2 + zl
            mine = aligned(self.base + me * self.chunk, self.chunk)
            for number in self.n_back:
                arrived(number, self.res.at[mine])
            if self.halves:
                half = aligned(self.base, 64)
                self.n_half = send(self.res.at[half], self.res.at[half], sibling)

        def done(self):
            if self.halves:
                arrived(self.n_half, self.res.at[aligned(self.base, 64)])

    gram = Total(gsrc, gk, ga, g7, gz, gx, gres, True)

    class Quick:
        def __init__(self, src, by_row, by_col, res):
            self.src, self.by_row, self.by_col, self.res = src, by_row, by_col, res

        def part(self, index):
            return aligned(index * 8, 8)

        def to_row(self):
            self.n = []
            for d in row_others:
                there = at_row(*d)
                self.n.append(
                    send(self.src.at[self.part(there[0])], self.by_row.at[r], there)
                )
            self.by_row[r] = self.src[self.part(r), :]

        def to_col(self):
            for number in self.n:
                arrived(number, self.by_row.at[r])
            total = self.by_row[0]
            for i in range(1, 16):
                total = total + self.by_row[i]
            self.by_col[c] = total
            mine = self.by_col.at[c]
            self.n = [send(mine, mine, at_col(*d)) for d in col_others]

        def back(self):
            for number in self.n:
                arrived(number, self.by_col.at[c])
            total = self.by_col[0]
            for i in range(1, 16):
                total = total + self.by_col[i]
            self.res[self.part(r), :] = total
            mine = self.res.at[self.part(r)]
            self.n = [send(mine, mine, at_row(*d)) for d in row_others]

        def done(self):
            for number in self.n:
                arrived(number, self.res.at[self.part(r)])

    quick = Quick(csrc, c16, cc, cres)
    steps["s0"], steps["s1"], steps["s2"], steps["s3"] = (
        quick.to_row,
        quick.to_col,
        quick.back,
        quick.done,
    )
    for index, name in enumerate(
        ("to_core", "to_row", "to_z", "to_x", "back_row", "back_core", "done")
    ):
        steps[f"g{index}"] = getattr(gram, name)

    def slot(x_step, z_step):
        return ((x + x_step) % 4) * 4 + (zh + z_step) % 4

    n_z = {}
    n_xup, n_xdown, n_xfup, n_xfdown = {}, {}, {}, {}

    def x_send(k, src):
        there = rowp.at[slot(0, k)]
        n_xup[k] = send(src, there, at_x(1))
        n_xdown[k] = send(src, there, at_x(3))

    def x_up(k):
        low = rowp.at[slot(3, k)]
        arrived(n_xup[k], low)
        n_xfup[k] = send(low.at[0:TOP], low.at[0:TOP], at_x(1))

    def x_down(k):
        high = rowp.at[slot(1, k)]
        arrived(n_xdown[k], high)
        n_xfdown[k] = send(high.at[TOP:ROWS], high.at[TOP:ROWS], at_x(3))

    def x_last(k):
        opposite = rowp.at[slot(2, k)]
        arrived(n_xfup[k], opposite.at[0:TOP])
        arrived(n_xfdown[k], opposite.at[TOP:ROWS])

    for k in range(4):
        steps[f"xf{k}u"] = lambda k=k: x_up(k)
        steps[f"xf{k}d"] = lambda k=k: x_down(k)
        steps[f"xl{k}"] = lambda k=k: x_last(k)

    @step
    def z0():
        n_z["up"] = send(geno_ref, rowp.at[c], at_z(1))
        n_z["down"] = send(geno_ref, rowp.at[c], at_z(3))

    @step
    def x0():
        x_send(0, geno_ref)

    @step
    def z1u():
        low = rowp.at[slot(0, 3)]
        arrived(n_z["up"], low)
        n_z["fup"] = send(low.at[0:TOP], low.at[0:TOP], at_z(1))
        x_send(3, low)

    @step
    def z1d():
        high = rowp.at[slot(0, 1)]
        arrived(n_z["down"], high)
        n_z["fdown"] = send(high.at[TOP:ROWS], high.at[TOP:ROWS], at_z(3))
        x_send(1, high)

    @step
    def z2():
        opposite = rowp.at[slot(0, 2)]
        arrived(n_z["fup"], opposite.at[0:TOP])
        arrived(n_z["fdown"], opposite.at[TOP:ROWS])
        x_send(2, opposite)

    def cslot(dy, dl, other=0):
        return row_of((y + dy) % 4, (zl + dl) % 2, (core + other) % 2)

    n_yup, n_ydown, n_yfup, n_yfdown, n_pair = {}, {}, {}, {}, {}
    n_zl = []

    def pair_send(dy, dl):
        block = cblock(cslot(dy, dl))
        n_pair[dy, dl] = send(block, block, sibling)

    def y_send(dl):
        block = cblock(cslot(0, dl))
        n_yup[dl] = send(block, block, at_y(1, 0))
        n_ydown[dl] = send(block, block, at_y(3, 0))
        pair_send(0, dl)

    def y_up(dl):
        low = cblock(cslot(3, dl))
        arrived(n_yup[dl], low)
        n_yfup[dl] = send(low.at[0:TOP], low.at[0:TOP], at_y(1, 0))
        pair_send(3, dl)

    def y_down(dl):
        high = cblock(cslot(1, dl))
        arrived(n_ydown[dl], high)
        n_yfdown[dl] = send(high.at[TOP:ROWS], high.at[TOP:ROWS], at_y(3, 0))
        pair_send(1, dl)

    def y_last(dl):
        opposite = cblock(cslot(2, dl))
        arrived(n_yfup[dl], opposite.at[0:TOP])
        arrived(n_yfdown[dl], opposite.at[TOP:ROWS])
        pair_send(2, dl)

    for dl in range(2):
        steps[f"yf{dl}u"] = lambda dl=dl: y_up(dl)
        steps[f"yf{dl}d"] = lambda dl=dl: y_down(dl)
        steps[f"yl{dl}"] = lambda dl=dl: y_last(dl)

    @step
    def m0():
        mirror_start("c")

    @step
    def m1():
        mirrored("c")
        n_zl.append(send(cblock(r), cblock(r), at_y(0, 1)))
        y_send(0)

    @step
    def m2():
        arrived(n_zl[0], cblock(cslot(0, 1)))
        y_send(1)

    @step
    def p():
        for dl in range(2):
            for dy in range(4):
                arrived(n_pair[dy, dl], cblock(cslot(dy, dl, 1)))

    n_t, n_tp, n_tz = [], {}, []

    @step
    def t0():
        mirror_start("t")

    @step
    def tz0():
        for i in (1, 2, 3):
            n_tz.append(send(traits_ref, tr.at[zh], at_z(i)))
        tr[zh] = traits[...]

    @step
    def tz1():
        for number in n_tz:
            arrived(number, tr.at[zh])

    @step
    def t1():
        mirrored("t")
        for dy, dl in others:
            n_t.append(send(tp.at[r], tp.at[r], at_y(dy, dl)))
        n_tp[0, 0] = send(tp.at[r], tp.at[r], sibling)

    @step
    def t2():
        for number, (dy, dl) in zip(n_t, others, strict=True):
            block = tp.at[cslot(-dy, -dl)]
            arrived(number, block)
            n_tp[-dy % 4, dl] = send(block, block, sibling)

    n_rsx, n_rsz = [], []

    @step
    def t3():
        for (dy, dl), number in n_tp.items():
            arrived(number, tp.at[cslot(dy, dl, 1)])
        load_rel.wait()
        t_high, t_low = split(tp[...].reshape(PANEL, PROT))
        tb[:, :PROT] = t_high
        tb[:, PROT:] = t_low

    def times_traits(i):
        rows = aligned(((x + i) % 4) * GROUP, GROUP)
        r_high, r_low = split(rel[rows, :])
        both = dot(r_high, tb[...], ((1,), (0,)))
        product = both[:, :PROT] + both[:, PROT:] + dot(r_low, tb[:, :PROT], ((1,), (0,)))
        zbuf[rows, :] = product
        if i:
            n_rsx.append(send(zbuf.at[rows], rsx.at[x], at_x(i)))
        else:
            rsx[x] = product

    for i in range(4):
        steps[f"m{i}t"] = lambda i=i: times_traits(i)

    @step
    def t4():
        for number in n_rsx:
            arrived(number, rsx.at[x])
        zsum[...] = (rsx[0] + rsx[1]) + (rsx[2] + rsx[3])
        for i in (1, 2, 3):
            rows = aligned(((zh + i) % 4) * ROWS, ROWS)
            n_rsz.append(send(zsum.at[rows], rsz.at[zh], at_z(i)))
        rsz[zh] = zsum[aligned(zh * ROWS, ROWS), :]

    @step
    def tc():
        four = tr[...].reshape(GROUP, PROT)
        csrc[...] = dot(four, zsum[...], ((0,), (0,)), HIGHEST)

    @step
    def h():
        def plain(step, _):
            rows = aligned(step * 128, 128)
            block = (colp[rows, :].astype(F32) - nearest).T
            turned[:, rows] = block.astype(BF16)
            return 0

        lax.fori_loop(0, PANEL // 128, plain, 0)

    def update(i):
        which = (x + i) % 4
        rows = aligned(which * GROUP, GROUP)
        block = rowp[pl.ds(4 * which, 4)].reshape(GROUP, SNPS).astype(F32)
        value = ((block - nearest) - offset) * weight
        high, low = split(value)
        shift = jnp.sum(value * offset, axis=1, keepdims=True)
        sums = dot(high, turned[...], ((1,), (0,))) + dot(low, turned[...], ((1,), (0,)))
        rel[rows, :] = rel[rows, :] + (sums - shift)

    for k in range(4):
        steps[f"u{k}"] = lambda k=k: update(k)

    @step
    def op():
        for number in n_rsz:
            arrived(number, rsz.at[zh])
        own = (rsz[0] + rsz[1]) + (rsz[2] + rsz[3])
        product = own + dot(scores, gres[...], ((1,), (1,)), HIGHEST) * (1.0 / SNPS)
        projected_ref[...] = product * math.sqrt(SNPS / SAMPLES)

    @step
    def og():
        whole = gres[...]
        cross_ref[...] = dot(whole, whole, ((1,), (1,)), HIGHEST) * (1.0 / SNPS)

    @step
    def oc():
        cross_ref[...] = (cres[...] + cross_ref[...]) * (1.0 / SAMPLES)

    order = ORDER
    for name in order:
        steps[name]()

    for moved in started:
        moved.wait_send()
    mirror_sent("t")
    mirror_sent("c")


def store_kernel(updated_ref, projected_ref, cross_ref, out_ref, proj_ref, cp_ref, sem):
    tile = PANEL // STORES
    moves = [
        pltpu.make_async_copy(projected_ref, proj_ref, sem.at[STORES]),
        pltpu.make_async_copy(cross_ref, cp_ref, sem.at[STORES + 1]),
    ]
    for i in range(STORES):
        rows = pl.ds(i * tile, tile)
        moves.append(pltpu.make_async_copy(updated_ref.at[rows], out_ref.at[rows], sem.at[i]))
    for move in moves:
        move.start()
    for move in moves:
        move.wait()


def on_device(genotypes, allele_counts, relatedness, protein_traits):
    vmem = pl.BlockSpec(memory_space=pltpu.VMEM)
    anywhere = pl.BlockSpec(memory_space=pl.ANY)
    like = jax.ShapeDtypeStruct
    f32 = lambda *shape: pltpu.VMEM(shape, F32)
    updated, projected, cross = pl.pallas_call(
        exchange_kernel,
        out_shape=(f32(PANEL, PANEL), f32(ROWS, PROT), f32(PROT, PROT)),
        in_specs=[anywhere] * 4,
        out_specs=(vmem,) * 3,
        scratch_shapes=[
            pltpu.VMEM((1, SNPS), jnp.int32),
            f32(ROWS, PROT),
            pltpu.VMEM((16, ROWS, SNPS), jnp.int32),
            pltpu.VMEM((PANEL, SNPS), jnp.int32),
            f32(16, ROWS, PROT),
            f32(4, ROWS, PROT),
            pltpu.VMEM((SNPS, PANEL), BF16),
            pltpu.VMEM((PANEL, 2 * PROT), BF16),
            f32(PANEL, PROT),
            f32(GROUP, PROT),
            f32(4, GROUP, PROT),
            f32(4, ROWS, PROT),
            f32(128, SNPS),
            f32(64, SNPS),
            f32(64, SNPS),
            f32(8, 8, SNPS),
            f32(4, 8, SNPS),
            f32(4, 8, SNPS),
            f32(128, SNPS),
            f32(PROT, PROT),
            f32(16, 8, PROT),
            f32(16, 8, PROT),
            f32(PROT, PROT),
            pltpu.SemaphoreType.DMA((NSEM,)),
            pltpu.SemaphoreType.DMA((NSEM,)),
            pltpu.SemaphoreType.DMA((6,)),
        ],
        compiler_params=pltpu.CompilerParams(
            collective_id=1, has_side_effects=True, vmem_limit_bytes=VMEM_LIMIT
        ),
        name="exchange",
    )(allele_counts.reshape(1, SNPS), genotypes, protein_traits, relatedness)
    return pl.pallas_call(
        store_kernel,
        out_shape=(
            like((PANEL, PANEL), F32),
            like((ROWS, PROT), F32),
            like((PROT, PROT), F32),
        ),
        in_specs=[vmem] * 3,
        out_specs=(anywhere,) * 3,
        scratch_shapes=[pltpu.SemaphoreType.DMA((STORES + 2,))],
        compiler_params=pltpu.CompilerParams(vmem_limit_bytes=16 * 2**20),
        name="store",
    )(updated, projected, cross)


def solution(mesh):
    in_specs = (P(("row", "col"), None), P(), P("row", "col"), P(("row", "col"), None))
    out_specs = (P("row", "col"), P(("row", "col"), None), P())
    return jax.shard_map(
        on_device, mesh=mesh, in_specs=in_specs, out_specs=out_specs, check_vma=False
    )
```

time: 83.7 us -> 67.7 us (0.81)
  Pallas kernels: 79.8 us -> 67 us
  local copies, waits for them, and re-layouts: 2.35 us -> 0 us
    pallas_call x2, Pallas kernels: 79.8 us -> 67 us  [the longest x1 64.5 us: on_device(): pl.pallas_call(exchange_kernel, out_shape=(f32(PANEL, PANEL), f32(ROWS, P...]
    unnamed x6 -> x0, local copies, waits for them, and re-layouts: 2.35 us -> none
where the time goes in v2:
time: 67.7 us; the launch traced here: 67.6 us
  Pallas kernels  67 us (99%)
    pallas_call x1, Pallas kernels, on_device(): pl.pallas_call(exchange_kernel, out_shape=(f32(PANEL, PANEL), f32(ROWS, P...  64.5 us
    pallas_call x1, Pallas kernels, on_device(): pl.pallas_call(store_kernel, out_shape=(like((PANEL, PANEL), F32), like((...  2.49 us

profile of v2, /device:TPU:1, one launch (start us, length us, event | category | flops | bytes accessed | tf_op | source)
XLA Modules:
  0.0 67.6 jit_solution(6306148222328665132)
XLA Ops:
  0.6 64.5 %exchange.1 = (f32[1152,1152]{1,0:T(8,128)S(1)}, f32[72,128]{1,0:T(8,128)S(1)}, f32[128,128]{1,0:T(8,128)S(1)}) custom-call(s32[1,512]{1,0:T(1,128)} %bitcast.1, s32[72,512]{1,0:T(8,128)} %geno_ref.1, f32[72,128]{1,0:T(8,128)} %traits_ref.1, f32[1152,1152]{1,0:T(8,128)} %rel_ref.1), custom_call_target="tpu_custom_call" | custom-call | tf_op jit(solution)/shard_map/exchange/pallas_call | solution.py:606
  65.1 2.5 %store.1 = (f32[1152,1152]{1,0:T(8,128)}, f32[72,128]{1,0:T(8,128)}, f32[128,128]{1,0:T(8,128)}) custom-call(f32[1152,1152]{1,0:T(8,128)S(1)} %get-tuple-element.6.updated_ref, f32[72,128]{1,0:T(8,128)S(1)} %get-tuple-element.7.projected_ref, f32[128,128]{1,0:T(8,128)S(1)} %get-tuple-element.8.cross_ref), custom_call_target="tpu_custom_call" | custom-call | tf_op jit(solution)/shard_map/store/pallas_call | solution.py:644

commit v3 on v2

--- a/solution.py
+++ b/solution.py
@@ -24,11 +24,12 @@
 STORES = 8
 VMEM_LIMIT = 52 * 2**20
 ORDER = (
-    "g0", "t0", "z0", "m0", "t1", "g1", "x0", "z1d", "m1", "z1u", "t2", "t3", "m2t", "yf0u",
-    "yf0d", "tz0", "g2", "m3t", "m1t", "m2", "yl0", "m0t", "g3", "z2", "t4", "yf1u", "tz1",
-    "yf1d", "xf1u", "tc", "s0", "xf3u", "yl1", "g4", "xf0d", "s1", "p", "h", "xf2d", "xf3d",
-    "xf2u", "g5", "u0", "xf0u", "u3", "xf1d", "g6", "og", "s2", "u1", "xl0", "xl2", "op", "xl1",
-    "xl3", "u2", "s3", "oc",
+    "t0", "z0", "m0", "g0", "t1", "rs", "x0", "z1u", "g1", "x3s", "m1", "ys0", "t2a", "z1d",
+    "x1s", "t2", "yf0d", "g2", "yf0u", "t3", "tz0", "m2t", "m1t", "m3t", "m2", "ys1", "yf1u",
+    "xf1u", "yl0", "yf1d", "xf0d", "pp11", "pp20", "m0t", "tz1", "xf3d", "pp31", "pp00", "g3",
+    "z2", "pp30", "pp01", "t4", "tc", "s0", "pp10", "yl1", "x2s", "g4", "pp21", "xf1d", "s1",
+    "g5", "p", "xf0u", "h", "xl1", "xf3u", "xf2u", "u3", "g6", "op", "xf2d", "u1", "s2", "xl0",
+    "u0", "og", "xl3", "xl2", "u2", "s3", "oc",
 )
 
 
@@ -69,6 +70,8 @@
     tr,
     turned,
     tb,
+    rh,
+    rl,
     zbuf,
     zsum,
     rsx,
@@ -119,7 +122,11 @@
         (dy, dl, dk) for dk in range(2) for dl in range(2) for dy in range(4)
     ][1:]
     col_others = [(dx, dz) for dz in range(4) for dx in range(4)][1:]
-    partners = [at_row(*d) for d in row_others] + [at_col(*d) for d in col_others]
+    partners = (
+        [at_row(*d) for d in row_others]
+        + [at_x(i) for i in (1, 2, 3)]
+        + [at_z(i) for i in (1, 2, 3)]
+    )
     far = r != c
 
     names = itertools.count()
@@ -386,21 +393,21 @@
         low = rowp.at[slot(0, 3)]
         arrived(n_z["up"], low)
         n_z["fup"] = send(low.at[0:TOP], low.at[0:TOP], at_z(1))
-        x_send(3, low)
 
     @step
     def z1d():
         high = rowp.at[slot(0, 1)]
         arrived(n_z["down"], high)
         n_z["fdown"] = send(high.at[TOP:ROWS], high.at[TOP:ROWS], at_z(3))
-        x_send(1, high)
 
     @step
     def z2():
         opposite = rowp.at[slot(0, 2)]
         arrived(n_z["fup"], opposite.at[0:TOP])
         arrived(n_z["fdown"], opposite.at[TOP:ROWS])
-        x_send(2, opposite)
+
+    for k in (1, 2, 3):
+        steps[f"x{k}s"] = lambda k=k: x_send(k, rowp.at[slot(0, k)])
 
     def cslot(dy, dl, other=0):
         return row_of((y + dy) % 4, (zl + dl) % 2, (core + other) % 2)
@@ -416,27 +423,26 @@
         block = cblock(cslot(0, dl))
         n_yup[dl] = send(block, block, at_y(1, 0))
         n_ydown[dl] = send(block, block, at_y(3, 0))
-        pair_send(0, dl)
 
     def y_up(dl):
         low = cblock(cslot(3, dl))
         arrived(n_yup[dl], low)
         n_yfup[dl] = send(low.at[0:TOP], low.at[0:TOP], at_y(1, 0))
-        pair_send(3, dl)
 
     def y_down(dl):
         high = cblock(cslot(1, dl))
         arrived(n_ydown[dl], high)
         n_yfdown[dl] = send(high.at[TOP:ROWS], high.at[TOP:ROWS], at_y(3, 0))
-        pair_send(1, dl)
 
     def y_last(dl):
         opposite = cblock(cslot(2, dl))
         arrived(n_yfup[dl], opposite.at[0:TOP])
         arrived(n_yfdown[dl], opposite.at[TOP:ROWS])
-        pair_send(2, dl)
 
     for dl in range(2):
+        steps[f"ys{dl}"] = lambda dl=dl: y_send(dl)
+        for dy in range(4):
+            steps[f"pp{dy}{dl}"] = lambda dy=dy, dl=dl: pair_send(dy, dl)
         steps[f"yf{dl}u"] = lambda dl=dl: y_up(dl)
         steps[f"yf{dl}d"] = lambda dl=dl: y_down(dl)
         steps[f"yl{dl}"] = lambda dl=dl: y_last(dl)
@@ -449,12 +455,10 @@
     def m1():
         mirrored("c")
         n_zl.append(send(cblock(r), cblock(r), at_y(0, 1)))
-        y_send(0)
 
     @step
     def m2():
         arrived(n_zl[0], cblock(cslot(0, 1)))
-        y_send(1)
 
     @step
     def p():
@@ -486,29 +490,40 @@
             n_t.append(send(tp.at[r], tp.at[r], at_y(dy, dl)))
         n_tp[0, 0] = send(tp.at[r], tp.at[r], sibling)
 
-    @step
-    def t2():
-        for number, (dy, dl) in zip(n_t, others, strict=True):
+    def t_pair(begin, end):
+        for number, (dy, dl) in list(zip(n_t, others, strict=True))[begin:end]:
             block = tp.at[cslot(-dy, -dl)]
             arrived(number, block)
             n_tp[-dy % 4, dl] = send(block, block, sibling)
 
+    steps["t2a"] = lambda: t_pair(0, 3)
+    steps["t2"] = lambda: t_pair(3, 7)
+
     n_rsx, n_rsz = [], []
 
     @step
     def t3():
         for (dy, dl), number in n_tp.items():
             arrived(number, tp.at[cslot(dy, dl, 1)])
-        load_rel.wait()
         t_high, t_low = split(tp[...].reshape(PANEL, PROT))
         tb[:, :PROT] = t_high
         tb[:, PROT:] = t_low
 
+    @step
+    def rs():
+        load_rel.wait()
+
+        def halve(i, _):
+            rows = aligned(i * 144, 144, 16)
+            rh[rows, :], rl[rows, :] = split(rel[rows, :])
+            return 0
+
+        lax.fori_loop(0, 8, halve, 0)
+
     def times_traits(i):
-        rows = aligned(((x + i) % 4) * GROUP, GROUP)
-        r_high, r_low = split(rel[rows, :])
-        both = dot(r_high, tb[...], ((1,), (0,)))
-        product = both[:, :PROT] + both[:, PROT:] + dot(r_low, tb[:, :PROT], ((1,), (0,)))
+        rows = aligned(((x + i) % 4) * GROUP, GROUP, 16)
+        both = dot(rh[rows, :], tb[...], ((1,), (0,)))
+        product = both[:, :PROT] + both[:, PROT:] + dot(rl[rows, :], tb[:, :PROT], ((1,), (0,)))
         zbuf[rows, :] = product
         if i:
             n_rsx.append(send(zbuf.at[rows], rsx.at[x], at_x(i)))
@@ -617,6 +632,8 @@
             f32(4, ROWS, PROT),
             pltpu.VMEM((SNPS, PANEL), BF16),
             pltpu.VMEM((PANEL, 2 * PROT), BF16),
+            pltpu.VMEM((PANEL, PANEL), BF16),
+            pltpu.VMEM((PANEL, PANEL), BF16),
             f32(PANEL, PROT),
             f32(GROUP, PROT),
             f32(4, GROUP, PROT),

time: 67.7 us -> 66.4 us (0.981)
  Pallas kernels: 67 us -> 65.6 us
    pallas_call x1, Pallas kernels: 64.5 us -> 63.1 us  [on_device(): pl.pallas_call(exchange_kernel, out_shape=(f32(PANEL, PANEL), f32(ROWS, P...]
where the time goes in v3:
time: 66.4 us; the launch traced here: 66.3 us
  Pallas kernels  65.6 us (99%)
    pallas_call x1, Pallas kernels, on_device(): pl.pallas_call(exchange_kernel, out_shape=(f32(PANEL, PANEL), f32(ROWS, P...  63.1 us
    pallas_call x1, Pallas kernels, on_device(): pl.pallas_call(store_kernel, out_shape=(like((PANEL, PANEL), F32), like((...  2.49 us

profile of v3, /device:TPU:1, one launch (start us, length us, event | category | flops | bytes accessed | tf_op | source)
XLA Modules:
  0.0 66.3 jit_solution(11513305516409933565)
XLA Ops:
  0.6 63.1 %exchange.1 = (f32[1152,1152]{1,0:T(8,128)S(1)}, f32[72,128]{1,0:T(8,128)S(1)}, f32[128,128]{1,0:T(8,128)S(1)}) custom-call(s32[1,512]{1,0:T(1,128)} %bitcast.1, s32[72,512]{1,0:T(8,128)} %geno_ref.1, f32[72,128]{1,0:T(8,128)} %traits_ref.1, f32[1152,1152]{1,0:T(8,128)} %rel_ref.1), custom_call_target="tpu_custom_call" | custom-call | tf_op jit(solution)/shard_map/exchange/pallas_call | solution.py:621
  63.8 2.5 %store.1 = (f32[1152,1152]{1,0:T(8,128)}, f32[72,128]{1,0:T(8,128)}, f32[128,128]{1,0:T(8,128)}) custom-call(f32[1152,1152]{1,0:T(8,128)S(1)} %get-tuple-element.6.updated_ref, f32[72,128]{1,0:T(8,128)S(1)} %get-tuple-element.7.projected_ref, f32[128,128]{1,0:T(8,128)S(1)} %get-tuple-element.8.cross_ref), custom_call_target="tpu_custom_call" | custom-call | tf_op jit(solution)/shard_map/store/pallas_call | solution.py:661

commit v4 on v3

--- a/solution.py
+++ b/solution.py
@@ -118,10 +118,13 @@
     def at_col(dx, dz):
         return (r, ((x + dx) % 4) * 4 + (zh + dz) % 4)
 
+    far_first = sorted(others, key=lambda d: -min(d[0], 4 - d[0]) - d[1])
     row_others = [
         (dy, dl, dk) for dk in range(2) for dl in range(2) for dy in range(4)
     ][1:]
     col_others = [(dx, dz) for dz in range(4) for dx in range(4)][1:]
+    col_others.sort(key=lambda d: -min(d[0], 4 - d[0]) - 2 * min(d[1], 4 - d[1]))
+    row_others.sort(key=lambda d: -min(d[0], 4 - d[0]) - d[1])
     partners = (
         [at_row(*d) for d in row_others]
         + [at_x(i) for i in (1, 2, 3)]
@@ -246,7 +249,7 @@
             self.acc[...] = mine + self.bk[...]
             me = y * 2 + zl
             self.n_row = []
-            for dy, dl in others:
+            for dy, dl in far_first:
                 q = ((y + dy) % 4) * 2 + (zl + dl) % 2
                 self.n_row.append(
                     send(self.acc.at[self.part(q)], self.b7.at[me], at_y(dy, dl))
@@ -261,14 +264,14 @@
             for i in range(1, 8):
                 total = total + self.b7[i]
             self.bz[zh] = total
-            self.n_z = [send(self.bz.at[zh], self.bz.at[zh], at_z(i)) for i in (1, 2, 3)]
+            self.n_z = [send(self.bz.at[zh], self.bz.at[zh], at_z(i)) for i in (2, 1, 3)]
 
         def to_x(self):
             for number in self.n_z:
                 arrived(number, self.bz.at[zh])
             total = (self.bz[0] + self.bz[1]) + (self.bz[2] + self.bz[3])
             self.bx[x] = total
-            self.n_x = [send(self.bx.at[x], self.bx.at[x], at_x(i)) for i in (1, 2, 3)]
+            self.n_x = [send(self.bx.at[x], self.bx.at[x], at_x(i)) for i in (2, 1, 3)]
 
         def back_row(self):
             for number in self.n_x:
@@ -278,7 +281,7 @@
             mine = aligned(self.base + me * self.chunk, self.chunk)
             self.res[mine, :] = total
             self.n_back = [
-                send(self.res.at[mine], self.res.at[mine], at_y(dy, dl)) for dy, dl in others
+                send(self.res.at[mine], self.res.at[mine], at_y(dy, dl)) for dy, dl in far_first
             ]
 
         def back_core(self):
@@ -474,7 +477,7 @@
 
     @step
     def tz0():
-        for i in (1, 2, 3):
+        for i in (2, 1, 3):
             n_tz.append(send(traits_ref, tr.at[zh], at_z(i)))
         tr[zh] = traits[...]
 
@@ -486,8 +489,8 @@
     @step
     def t1():
         mirrored("t")
-        for dy, dl in others:
-            n_t.append(send(tp.at[r], tp.at[r], at_y(dy, dl)))
+        sent = {d: send(tp.at[r], tp.at[r], at_y(*d)) for d in far_first}
+        n_t.extend(sent[d] for d in others)
         n_tp[0, 0] = send(tp.at[r], tp.at[r], sibling)
 
     def t_pair(begin, end):

time: 66.4 us -> 65.5 us (0.986)
  Pallas kernels: 65.6 us -> 64.7 us
    pallas_call x1, Pallas kernels: 63.1 us -> 62.2 us  [on_device(): pl.pallas_call(exchange_kernel, out_shape=(f32(PANEL, PANEL), f32(ROWS, P...]
where the time goes in v4:
time: 65.5 us; the launch traced here: 65.3 us
  Pallas kernels  64.7 us (99%)
    pallas_call x1, Pallas kernels, on_device(): pl.pallas_call(exchange_kernel, out_shape=(f32(PANEL, PANEL), f32(ROWS, P...  62.2 us
    pallas_call x1, Pallas kernels, on_device(): pl.pallas_call(store_kernel, out_shape=(like((PANEL, PANEL), F32), like((...  2.49 us

profile of v4, /device:TPU:1, one launch (start us, length us, event | category | flops | bytes accessed | tf_op | source)
XLA Modules:
  0.0 65.3 jit_solution(7941887861552406371)
XLA Ops:
  0.6 62.2 %exchange.1 = (f32[1152,1152]{1,0:T(8,128)S(1)}, f32[72,128]{1,0:T(8,128)S(1)}, f32[128,128]{1,0:T(8,128)S(1)}) custom-call(s32[1,512]{1,0:T(1,128)} %bitcast.1, s32[72,512]{1,0:T(8,128)} %geno_ref.1, f32[72,128]{1,0:T(8,128)} %traits_ref.1, f32[1152,1152]{1,0:T(8,128)} %rel_ref.1), custom_call_target="tpu_custom_call" | custom-call | tf_op jit(solution)/shard_map/exchange/pallas_call | solution.py:624
  62.9 2.5 %store.1 = (f32[1152,1152]{1,0:T(8,128)}, f32[72,128]{1,0:T(8,128)}, f32[128,128]{1,0:T(8,128)}) custom-call(f32[1152,1152]{1,0:T(8,128)S(1)} %get-tuple-element.6.updated_ref, f32[72,128]{1,0:T(8,128)S(1)} %get-tuple-element.7.projected_ref, f32[128,128]{1,0:T(8,128)S(1)} %get-tuple-element.8.cross_ref), custom_call_target="tpu_custom_call" | custom-call | tf_op jit(solution)/shard_map/store/pallas_call | solution.py:664

commit v5 on v4

--- a/solution.py
+++ b/solution.py
@@ -28,7 +28,7 @@
     "x1s", "t2", "yf0d", "g2", "yf0u", "t3", "tz0", "m2t", "m1t", "m3t", "m2", "ys1", "yf1u",
     "xf1u", "yl0", "yf1d", "xf0d", "pp11", "pp20", "m0t", "tz1", "xf3d", "pp31", "pp00", "g3",
     "z2", "pp30", "pp01", "t4", "tc", "s0", "pp10", "yl1", "x2s", "g4", "pp21", "xf1d", "s1",
-    "g5", "p", "xf0u", "h", "xl1", "xf3u", "xf2u", "u3", "g6", "op", "xf2d", "u1", "s2", "xl0",
+    "g5", "p", "xf0u", "h", "xl1", "xf3u", "xf2u", "xf2d", "u3", "g6", "op", "u1", "s2", "xl0",
     "u0", "og", "xl3", "xl2", "u2", "s3", "oc",
 )
 

time: 65.5 us -> 65.5 us (level)
  no operation moved by 1% of the time
where the time goes in v5:
time: 65.5 us; the launch traced here: 65.3 us
  Pallas kernels  64.7 us (99%)
    pallas_call x1, Pallas kernels, on_device(): pl.pallas_call(exchange_kernel, out_shape=(f32(PANEL, PANEL), f32(ROWS, P...  62.2 us
    pallas_call x1, Pallas kernels, on_device(): pl.pallas_call(store_kernel, out_shape=(like((PANEL, PANEL), F32), like((...  2.49 us

profile of v5, /device:TPU:1, one launch (start us, length us, event | category | flops | bytes accessed | tf_op | source)
XLA Modules:
  0.0 65.3 jit_solution(3764145121068030240)
XLA Ops:
  0.6 62.2 %exchange.1 = (f32[1152,1152]{1,0:T(8,128)S(1)}, f32[72,128]{1,0:T(8,128)S(1)}, f32[128,128]{1,0:T(8,128)S(1)}) custom-call(s32[1,512]{1,0:T(1,128)} %bitcast.1, s32[72,512]{1,0:T(8,128)} %geno_ref.1, f32[72,128]{1,0:T(8,128)} %traits_ref.1, f32[1152,1152]{1,0:T(8,128)} %rel_ref.1), custom_call_target="tpu_custom_call" | custom-call | tf_op jit(solution)/shard_map/exchange/pallas_call | solution.py:624
  62.9 2.5 %store.1 = (f32[1152,1152]{1,0:T(8,128)}, f32[72,128]{1,0:T(8,128)}, f32[128,128]{1,0:T(8,128)}) custom-call(f32[1152,1152]{1,0:T(8,128)S(1)} %get-tuple-element.6.updated_ref, f32[72,128]{1,0:T(8,128)S(1)} %get-tuple-element.7.projected_ref, f32[128,128]{1,0:T(8,128)S(1)} %get-tuple-element.8.cross_ref), custom_call_target="tpu_custom_call" | custom-call | tf_op jit(solution)/shard_map/store/pallas_call | solution.py:664
